TPU v7x, 32 devices: a whole 2x2x4 slice. The times are simulated.
32 devices in a mesh: groups: 2 (over y), seq: 4 (over z), strand: 2 (over core), chan: 2 (over x).
Axes of the slice: x: 2, y: 2, z: 4, core: 2. Of those that a mesh axis runs over, the one named last changes fastest.
Arguments:
- seq_in: bfloat16 [2, 6144, 512], P('strand', ('groups', 'seq', 'chan')), parts along dimension 1, may hold values from -6 to 6
- conv_norm: float32 [2, 512], replicated, may hold values from 0.1 to 1.9
- conv_weight: bfloat16 [2, 3, 512, 512], P(None, None, None, ('seq', 'chan')), may hold values from -0.15625 to 0.15625
- ff_norm: float32 [2, 512], replicated, may hold values from 0.1 to 1.9
- up_weight: bfloat16 [2, 512, 2048], P(None, None, ('seq', 'chan')), may hold values from -0.25 to 0.25
- down_weight: bfloat16 [2, 2048, 512], P(None, ('seq', 'chan')), may hold values from -0.125 to 0.125
- head_norm: float32 [512], replicated, may hold values from 0.1 to 1.9
- value_weight: bfloat16 [512, 512], replicated, may hold values from -0.25 to 0.25
- gate_weight: bfloat16 [512, 512], replicated, may hold values from -0.25 to 0.25
- out_weight: bfloat16 [512, 512], replicated, may hold values from -0.25 to 0.25
Outputs:
- strand_out: bfloat16 [2, 6144, 512], P('strand', ('groups', 'seq', 'chan')), parts along dimension 1
There are 2 independent parts, one for each index of `groups`. A program takes and returns all parts, laid end to end along the dimension named above; an argument that names none is the same for every part. Nothing has to cross between parts.
All inputs are finite; a program needn't handle non-finite values.
Results may differ from a plain program's by a relative error of at most 0.015.
Values may be sent and summed in bfloat16 or wider, within the bound.
A program may use at most 64 MiB of HBM per device.

v0:
```python
import jax
import jax.numpy as jnp
from jax import lax
from jax.sharding import PartitionSpec as P


def passed_along(value, axis, steps):
    count = lax.axis_size(axis)
    initial, last = (max(0, -steps), min(count, count - steps))
    return lax.ppermute(value, axis, [(source, source + steps) for source in range(initial, last)])


def swapped(x, axis, stride):
    return lax.ppermute(x, axis, [(i, i ^ 1 << stride) for i in range(lax.axis_size(axis))])


def normalize(values, gain):
    return values * lax.rsqrt(jnp.mean(values * values, axis=-1, keepdims=True) + 1e-06) * gain


def matmul(left, right):
    return jnp.dot(left, right, preferred_element_type=jnp.float32)


def local(
    seq_in,
    conv_norm,
    conv_weight,
    ff_norm,
    up_weight,
    down_weight,
    head_norm,
    value_weight,
    gate_weight,
    out_weight,
):
    state = seq_in[0].astype(jnp.float32)
    seq_count = lax.axis_size("seq")
    for block in range(conv_weight.shape[0]):
        reach = min(2**block, seq_count // 2)
        normed = normalize(state, conv_norm[block]).astype(jnp.bfloat16)
        before = passed_along(normed, "seq", reach)
        after = passed_along(normed, "seq", -reach)
        piece = lax.all_gather(conv_weight[block], ("seq", "chan"), axis=2, tiled=True)
        total = matmul(before, piece[0]) + matmul(normed, piece[1]) + matmul(after, piece[2])
        conv = total.astype(jnp.bfloat16)
        state = state + conv.astype(jnp.float32)
        mixed = normalize(state, ff_norm[block]).astype(jnp.bfloat16)
        hidden = jax.nn.gelu(
            matmul(mixed, lax.all_gather(up_weight[block], ("seq", "chan"), axis=1, tiled=True))
        ).astype(jnp.bfloat16)
        state = state + matmul(
            hidden, lax.all_gather(down_weight[block], ("seq", "chan"), axis=0, tiled=True)
        )
    final = normalize(state, head_norm).astype(jnp.bfloat16)
    value = matmul(final, value_weight)
    bit_count = (seq_count * lax.axis_size("chan")).bit_length() - 1
    opposite = swapped(final, "strand", 0)
    for digit in range(bit_count):
        opposite = swapped(opposite, ("seq", "chan"), digit)
    opposite = jnp.flip(opposite, 0)
    mirrored = matmul(opposite, gate_weight).astype(jnp.bfloat16)
    gated = (value * jax.nn.sigmoid(mirrored.astype(jnp.float32))).astype(jnp.bfloat16)
    result = matmul(gated, out_weight)
    return result.astype(jnp.bfloat16)[None]


def solution(mesh):
    in_specs = (
        P("strand", ("groups", "seq", "chan"), None),
        P(),
        P(None, None, None, ("seq", "chan")),
        P(),
        P(None, None, ("seq", "chan")),
        P(None, ("seq", "chan"), None),
        P(),
        P(),
        P(),
        P(),
    )
    out_specs = P("strand", ("groups", "seq", "chan"), None)
    return jax.shard_map(local, mesh=mesh, in_specs=in_specs, out_specs=out_specs, check_vma=False)
```

profile of v0, /device:TPU:0, one launch (start us, length us, event | category | flops | bytes accessed | tf_op | source)
XLA Modules:
  0.0 376.3 jit_solution(10085259237027235437)
XLA Ops:
  6.5 0.0 all-gather.13.cloned.1.call-start
  6.6 1.9 fusion.86
  8.5 0.0 all-gather.15.cloned.1.call-start
  8.6 1.9 fusion.84
  10.5 0.0 all-gather.17.cloned.1.call-start
  10.5 0.8 fusion.85
  11.4 0.0 all-gather.19.cloned.1.call-start
  11.4 0.5 all-gather.19.cloned.1.call-update
  12.0 0.0 all-gather.21.cloned.1.call-start
  12.0 0.5 all-gather.21.cloned.1.call-update
  12.6 0.0 all-gather.23.cloned.1.call-start
  12.6 0.2 fusion.55
  12.8 0.2 fusion.57
  13.0 1.3 collective-permute-start.1
  14.3 0.0 all-gather.23.cloned.1.call-update
  14.3 5.6 %collective-permute-start = (bf16[384,512]{1,0:T(8,128)(2,1)S(1)}, bf16[384,512]{1,0:T(8,128)(2,1)S(1)}, u32[]{:S(2)}, u32[]{:S(2)}) collective-permute-start(bf16[384,512]{1,0:T(8,128)(2,1)S(1)} %fusion.57), channel_id=1, source_target_pairs={{0,4},{4,8},{8,12},{1,5},{5,9},{9,13},{2,6},{6,10},{10,14},{3,7},{... | collective-permute-start | bytes 1179656 | tf_op jit(solution)/shard_map/ppermute | solution.py:10
  19.9 10.7 %collective-permute-done.1 = bf16[384,512]{1,0:T(8,128)(2,1)S(1)} collective-permute-done((bf16[384,512]{1,0:T(8,128)(2,1)S(1)}, bf16[384,512]{1,0:T(8,128)(2,1)S(1)}, u32[]{:S(2)}, u32[]{:S(2)}) %collective-permute-start.1) | collective-permute-done | bytes 393248 | tf_op jit(solution)/shard_map/ppermute | solution.py:10
  30.6 28.5 %all-gather.13.cloned.1.call-done = bf16[1,3,512,512]{2,3,1,0:T(8,128)(2,1)} async-done(((bf16[1,3,512,64]{2,3,1,0:T(8,128)(2,1)}), bf16[1,3,512,512]{2,3,1,0:T(8,128)(2,1)}) %all-gather.13.cloned.1.call-update) | async-done | bytes 1572880 | tf_op jit(solution)/shard_map/all_gather | solution.py:44
  59.0 1.4 fusion.62
  60.5 1.5 fusion.63
  62.0 1.6 multiply_reduce_fusion.3
  63.6 47.5 %all-gather.15.cloned.1.call-done = bf16[1,512,2048]{2,1,0:T(8,128)(2,1)} async-done(((bf16[1,512,256]{2,1,0:T(8,128)(2,1)}), bf16[1,512,2048]{2,1,0:T(8,128)(2,1)}) %all-gather.15.cloned.1.call-update) | async-done | bytes 2097168 | tf_op jit(solution)/shard_map/all_gather | solution.py:50
  111.0 49.6 %all-gather.17.cloned.1.call-done = bf16[1,2048,512]{2,1,0:T(8,128)(2,1)} async-done(((bf16[1,256,512]{2,1,0:T(8,128)(2,1)}), bf16[1,2048,512]{2,1,0:T(8,128)(2,1)}) %all-gather.17.cloned.1.call-update) | async-done | bytes 2097168 | tf_op jit(solution)/shard_map/all_gather | solution.py:53
  160.7 4.4 %multiply_reduce_fusion.2 = (f32[384]{0:T(512)S(1)}, f32[384,512]{1,0:T(8,128)S(1)}) fusion(f32[384,512]{1,0:T(8,128)S(1)} %get-tuple-element.16, bf16[1,2048,512]{2,1,0:T(8,128)(2,1)} %all-gather.17.cloned.1.call-done, bf16[1,512,2048]{2,1,0:T(8,128)(2,1)} %all-gather.15.cloned.1.call-done, f32[512]{0:T(512)S(1)} %bitcast.91, f32[384]{0:T(512)S(1)} %add_rsqrt_fusion.3), kind=kOutput, calls=%fused_computation.62 | convolution fusion | flops 1618869888 | bytes 5772288 | tf_op jit(solution)/shard_map/dot_general | solution.py:22
  165.0 0.1 multiply_convert_fusion.4
  165.2 1.3 collective-permute-start.3
  166.5 5.5 %collective-permute-start.2 = (bf16[384,512]{1,0:T(8,128)(2,1)S(1)}, bf16[384,512]{1,0:T(8,128)(2,1)S(1)}, u32[]{:S(2)}, u32[]{:S(2)}) collective-permute-start(bf16[384,512]{1,0:T(8,128)(2,1)S(1)} %multiply_convert_fusion.4), channel_id=1, source_target_pairs={{0,8},{4,12},{1,9},{5,13},{2,10},{6,14},{3,11},{7,15},{16,24},{20,... | collective-permute-start | bytes 1179656 | tf_op jit(solution)/shard_map/ppermute | solution.py:10
  172.0 46.6 %all-gather.19.cloned.1.call-done = bf16[1,3,512,512]{2,3,1,0:T(8,128)(2,1)} async-done(((bf16[1,3,512,64]{2,3,1,0:T(8,128)(2,1)}), bf16[1,3,512,512]{2,3,1,0:T(8,128)(2,1)}) %all-gather.19.cloned.1.call-update) | async-done | bytes 1572880 | tf_op jit(solution)/shard_map/all_gather | solution.py:44
  218.6 1.4 fusion.61
  220.1 1.4 fusion.60
  221.5 1.6 multiply_reduce_fusion.1
  223.1 47.3 %all-gather.21.cloned.1.call-done = bf16[1,512,2048]{2,1,0:T(8,128)(2,1)} async-done(((bf16[1,512,256]{2,1,0:T(8,128)(2,1)}), bf16[1,512,2048]{2,1,0:T(8,128)(2,1)}) %all-gather.21.cloned.1.call-update) | async-done | bytes 2097168 | tf_op jit(solution)/shard_map/all_gather | solution.py:50
  270.4 49.5 %all-gather.23.cloned.1.call-done = bf16[1,2048,512]{2,1,0:T(8,128)(2,1)} async-done(((bf16[1,256,512]{2,1,0:T(8,128)(2,1)}), bf16[1,2048,512]{2,1,0:T(8,128)(2,1)}) %all-gather.23.cloned.1.call-update) | async-done | bytes 2097168 | tf_op jit(solution)/shard_map/all_gather | solution.py:53
  319.9 4.4 %multiply_reduce_fusion = (f32[384]{0:T(512)S(1)}, f32[384,512]{1,0:T(8,128)S(1)}) fusion(f32[384,512]{1,0:T(8,128)S(1)} %get-tuple-element.20, bf16[1,2048,512]{2,1,0:T(8,128)(2,1)} %all-gather.23.cloned.1.call-done, bf16[1,512,2048]{2,1,0:T(8,128)(2,1)} %all-gather.21.cloned.1.call-done, f32[512]{0:T(512)S(1)} %bitcast.90, f32[384]{0:T(512)S(1)} %add_rsqrt_fusion.1), kind=kOutput, calls=%fused_computation.58 | convolution fusion | flops 1618869888 | bytes 5772288 | tf_op jit(solution)/shard_map/dot_general | solution.py:22
  324.3 0.1 multiply_convert_fusion
  324.4 0.1 collective-permute-start.4
  324.5 1.7 collective-permute-done.4
  326.2 0.6 collective-permute-start.5
  326.8 10.6 %collective-permute-done.5 = bf16[384,512]{1,0:T(8,128)(2,1)S(1)} collective-permute-done((bf16[384,512]{1,0:T(8,128)(2,1)S(1)}, bf16[384,512]{1,0:T(8,128)(2,1)S(1)}, u32[]{:S(2)}, u32[]{:S(2)}) %collective-permute-start.5) | collective-permute-done | bytes 393248 | tf_op jit(solution)/shard_map/ppermute | solution.py:14
  337.4 1.5 collective-permute-start.6
  338.8 8.8 %collective-permute-done.6 = bf16[384,512]{1,0:T(8,128)(2,1)S(1)} collective-permute-done((bf16[384,512]{1,0:T(8,128)(2,1)S(1)}, bf16[384,512]{1,0:T(8,128)(2,1)S(1)}, u32[]{:S(2)}, u32[]{:S(2)}) %collective-permute-start.6) | collective-permute-done | bytes 393248 | tf_op jit(solution)/shard_map/ppermute | solution.py:14
  347.7 1.8 collective-permute-start.7
  349.5 16.9 %collective-permute-done.7 = bf16[384,512]{1,0:T(8,128)(2,1)S(1)} collective-permute-done((bf16[384,512]{1,0:T(8,128)(2,1)S(1)}, bf16[384,512]{1,0:T(8,128)(2,1)S(1)}, u32[]{:S(2)}, u32[]{:S(2)}) %collective-permute-start.7) | collective-permute-done | bytes 393248 | tf_op jit(solution)/shard_map/ppermute | solution.py:14
  366.4 0.5 rev.4
  366.9 0.5 fusion.47
  367.4 0.5 copy-done.2
  367.9 0.2 copy-done.3
  368.1 1.4 fusion.48
  (27 shorter events, 0.1 us)
Async XLA Ops:
  6.5 360.4 %copy-start = (bf16[512,512]{1,0:T(8,128)(2,1)S(1)}, bf16[512,512]{1,0:T(8,128)(2,1)}, u32[]{:S(2)}) copy-start(bf16[512,512]{1,0:T(8,128)(2,1)} %param.18) | copy-start | bytes 1572868
  6.5 4.0 %copy-start.4 = (bf16[2,256,512]{2,1,0:T(8,128)(2,1)S(1)}, bf16[2,256,512]{2,1,0:T(8,128)(2,1)}, u32[]{:S(2)}) copy-start(bf16[2,256,512]{2,1,0:T(8,128)(2,1)} %param.15) | copy-start | bytes 1572868
  6.5 6.1 %copy-start.1 = (bf16[1,384,512]{2,1,0:T(8,128)(2,1)S(1)}, bf16[1,384,512]{2,1,0:T(8,128)(2,1)}, u32[]{:S(2)}) copy-start(bf16[1,384,512]{2,1,0:T(8,128)(2,1)} %param.10) | copy-start | bytes 1179652
  6.5 6.2 %copy-start.5 = (f32[2,512]{1,0:T(2,128)S(1)}, f32[2,512]{1,0:T(2,128)}, u32[]{:S(2)}) copy-start(f32[2,512]{1,0:T(2,128)} %param.11) | copy-start | bytes 12292
  6.5 52.5 %all-gather.13.cloned.1.call-start = ((), (), s32[]{:S(2)}) async-start(), calls=%async_computation | async-start | bytes 1769472 | tf_op jit(solution)/shard_map/all_gather | solution.py:44
  8.5 11.3 %copy-start.6 = (f32[2,512]{1,0:T(2,128)S(1)}, f32[2,512]{1,0:T(2,128)}, u32[]{:S(2)}) copy-start(f32[2,512]{1,0:T(2,128)} %param.13) | copy-start | bytes 12292
  8.5 102.5 %all-gather.15.cloned.1.call-start = ((), (), s32[]{:S(2)}) async-start(), calls=%async_computation.1 | async-start | bytes 2359296 | tf_op jit(solution)/shard_map/all_gather | solution.py:50
  10.5 150.2 %all-gather.17.cloned.1.call-start = ((), (), s32[]{:S(2)}) async-start(), calls=%async_computation.2 | async-start | bytes 2359296 | tf_op jit(solution)/shard_map/all_gather | solution.py:53
  11.4 207.2 %all-gather.19.cloned.1.call-start = ((), (), s32[]{:S(2)}) async-start(), calls=%async_computation.3 | async-start | bytes 1769472 | tf_op jit(solution)/shard_map/all_gather | solution.py:44
  12.0 258.4 %all-gather.21.cloned.1.call-start = ((), (), s32[]{:S(2)}) async-start(), calls=%async_computation.4 | async-start | bytes 2359296 | tf_op jit(solution)/shard_map/all_gather | solution.py:50
  12.6 307.3 %all-gather.23.cloned.1.call-start = ((), (), s32[]{:S(2)}) async-start(), calls=%async_computation.5 | async-start | bytes 2359296 | tf_op jit(solution)/shard_map/all_gather | solution.py:53
  13.0 17.6 %collective-permute-start.1 = (bf16[384,512]{1,0:T(8,128)(2,1)S(1)}, bf16[384,512]{1,0:T(8,128)(2,1)S(1)}, u32[]{:S(2)}, u32[]{:S(2)}) collective-permute-start(bf16[384,512]{1,0:T(8,128)(2,1)S(1)} %fusion.57), channel_id=1, source_target_pairs={{4,0},{8,4},{12,8},{5,1},{9,5},{13,9},{6,2},{10,6},{14,10},{7,3},{... | collective-permute-start | bytes 1179656 | tf_op jit(solution)/shard_map/ppermute | solution.py:10
  14.3 47.7 %collective-permute-start = (bf16[384,512]{1,0:T(8,128)(2,1)S(1)}, bf16[384,512]{1,0:T(8,128)(2,1)S(1)}, u32[]{:S(2)}, u32[]{:S(2)}) collective-permute-start(bf16[384,512]{1,0:T(8,128)(2,1)S(1)} %fusion.57), channel_id=1, source_target_pairs={{0,4},{4,8},{8,12},{1,5},{5,9},{9,13},{2,6},{6,10},{10,14},{3,7},{... | collective-permute-start | bytes 1179656 | tf_op jit(solution)/shard_map/ppermute | solution.py:10
  165.2 54.9 %collective-permute-start.3 = (bf16[384,512]{1,0:T(8,128)(2,1)S(1)}, bf16[384,512]{1,0:T(8,128)(2,1)S(1)}, u32[]{:S(2)}, u32[]{:S(2)}) collective-permute-start(bf16[384,512]{1,0:T(8,128)(2,1)S(1)} %multiply_convert_fusion.4), channel_id=1, source_target_pairs={{8,0},{12,4},{9,1},{13,5},{10,2},{14,6},{11,3},{15,7},{24,16},{28,... | collective-permute-start | bytes 1179656 | tf_op jit(solution)/shard_map/ppermute | solution.py:10
  166.5 55.0 %collective-permute-start.2 = (bf16[384,512]{1,0:T(8,128)(2,1)S(1)}, bf16[384,512]{1,0:T(8,128)(2,1)S(1)}, u32[]{:S(2)}, u32[]{:S(2)}) collective-permute-start(bf16[384,512]{1,0:T(8,128)(2,1)S(1)} %multiply_convert_fusion.4), channel_id=1, source_target_pairs={{0,8},{4,12},{1,9},{5,13},{2,10},{6,14},{3,11},{7,15},{16,24},{20,... | collective-permute-start | bytes 1179656 | tf_op jit(solution)/shard_map/ppermute | solution.py:10
  319.9 4.4 %copy-start.7 = (f32[512]{0:T(512)S(1)}, f32[512]{0:T(512)}, u32[]{:S(2)}) copy-start(f32[512]{0:T(512)} %param.16) | copy-start | bytes 6148
  324.4 1.8 collective-permute-start.4
  326.2 11.2 %collective-permute-start.5 = (bf16[384,512]{1,0:T(8,128)(2,1)S(1)}, bf16[384,512]{1,0:T(8,128)(2,1)S(1)}, u32[]{:S(2)}, u32[]{:S(2)}) collective-permute-start(bf16[384,512]{1,0:T(8,128)(2,1)S(1)} %collective-permute-done.4), channel_id=1, source_target_pairs={{0,1},{1,0},{4,5},{5,4},{8,9},{9,8},{12,13},{13,12},{2,3},{3,2},{6... | collective-permute-start | bytes 1179656 | tf_op jit(solution)/shard_map/ppermute | solution.py:14
  337.4 10.3 %collective-permute-start.6 = (bf16[384,512]{1,0:T(8,128)(2,1)S(1)}, bf16[384,512]{1,0:T(8,128)(2,1)S(1)}, u32[]{:S(2)}, u32[]{:S(2)}) collective-permute-start(bf16[384,512]{1,0:T(8,128)(2,1)S(1)} %collective-permute-done.5), channel_id=1, source_target_pairs={{0,4},{1,5},{4,0},{5,1},{8,12},{9,13},{12,8},{13,9},{2,6},{3,7},{6... | collective-permute-start | bytes 1179656 | tf_op jit(solution)/shard_map/ppermute | solution.py:14
  347.7 18.7 %collective-permute-start.7 = (bf16[384,512]{1,0:T(8,128)(2,1)S(1)}, bf16[384,512]{1,0:T(8,128)(2,1)S(1)}, u32[]{:S(2)}, u32[]{:S(2)}) collective-permute-start(bf16[384,512]{1,0:T(8,128)(2,1)S(1)} %collective-permute-done.6), channel_id=1, source_target_pairs={{0,8},{1,9},{4,12},{5,13},{8,0},{9,1},{12,4},{13,5},{2,10},{3,11},... | collective-permute-start | bytes 1179656 | tf_op jit(solution)/shard_map/ppermute | solution.py:14
  366.9 1.0 copy-start.2
  366.9 1.2 copy-start.3
Sparse Core Ops, SparseCore 0:
  9.6 49.4 all-gather.12
  61.1 49.8 all-gather.14
  113.1 47.4 all-gather.16
  162.7 55.8 all-gather.18
  220.5 49.8 all-gather.20
  272.4 47.4 all-gather.22
where the time goes:
time: 377 us; the launch traced here: 376 us
  waiting for transfers between devices  319 us (85%)
  matrix products  19.5 us (5%)
  starting transfers between devices  17.8 us (5%)
  between operations  13.7 us (4%)
  local copies, waits for them, and re-layouts  5.8 us (2%)
    all_gather x2, waiting for transfers between devices, local(): lax.all_gather(down_weight[block], ('seq', 'chan'), axis=0, tiled=True)  99.1 us
    all_gather x2, waiting for transfers between devices, local(): lax.all_gather(up_weight[block], ('seq', 'chan'), axis=1, tiled=True)  94.8 us
    all_gather x2, waiting for transfers between devices, local(): lax.all_gather(conv_weight[block], ('seq', 'chan'), axis=2, tiled=True)  75.1 us
    ppermute x4, waiting for transfers between devices, swapped(): lax.ppermute(x, axis, [(i, i ^ 1 << stride) for i in range(lax.axis_size(...  38.1 us
    dot_general x10, matrix products, matmul(): return jnp.dot(left, right, preferred_element_type=jnp.float32)  19.5 us
    ppermute x4, starting transfers between devices, passed_along(): lax.ppermute(value, axis, [(source, source + steps) for source in range(i...  13.7 us
    ppermute x4, waiting for transfers between devices, passed_along(): lax.ppermute(value, axis, [(source, source + steps) for source in range(i...  10.7 us
  transfers between devices with their start and end apart: 14, of which 11 were waited for; matrix products, arithmetic and copies ran while one was open for 4% of the time, Pallas kernels for 0%

commit v1 on v0

--- a/solution.py
+++ b/solution.py
@@ -1,6 +1,10 @@
+import functools
+
 import jax
 import jax.numpy as jnp
 from jax import lax
+from jax.experimental import pallas as pl
+from jax.experimental.pallas import tpu as pltpu
 from jax.sharding import PartitionSpec as P
 
 
@@ -65,6 +69,313 @@
     return result.astype(jnp.bfloat16)[None]
 
 
+def dot_t(left, right):
+    return lax.dot_general(left, right, (((1,), (1,)), ((), ())), preferred_element_type=jnp.float32)
+
+
+def fused_kernel(
+    nz,
+    nx,
+    seq_ref,
+    conv_norm,
+    conv_ref,
+    ff_norm,
+    up_ref,
+    down_ref,
+    head_norm,
+    value_ref,
+    gate_ref,
+    out_weight,
+    out_ref,
+    conv_all,
+    up_all,
+    down_all,
+    state,
+    acc,
+    hidden,
+    rows,
+    final,
+    opposite,
+    send_sem,
+    recv_sem,
+    row_send,
+    row_recv,
+    last_send,
+    last_recv,
+):
+    y, z, c, x = (lax.axis_index(a) for a in ("groups", "seq", "strand", "chan"))
+    blocks = conv_ref.shape[0]
+    owners = nz * nx
+    me = z * nx + x
+    count = rows.shape[2]
+    mirror = {"seq": nz - 1 - z, "strand": 1 - c, "chan": nx - 1 - x}
+    z_peer = [{"seq": lax.rem(z + d, nz)} for d in range(1, nz)]
+    x_peer, y_peer, c_peer = {"chan": 1 - x}, {"groups": 1 - y}, {"strand": 1 - c}
+    z_from = [lax.rem(z + nz - d, nz) for d in range(1, nz)]
+
+    partners = z_peer + [x_peer, y_peer, c_peer, mirror]
+    barrier = pltpu.get_barrier_semaphore()
+    for peer in partners:
+        pl.semaphore_signal(barrier, inc=1, device_id=peer, device_id_type=pl.DeviceIdType.MESH)
+
+    segments = []
+    for b in range(blocks):
+        for kind, (whole, own) in enumerate(((conv_all, conv_ref), (up_all, up_ref), (down_all, down_ref))):
+            whole[b, me] = own[b]
+            segments.append((kind, b, whole.at[b]))
+
+    def half(s, owner, core):
+        ref = segments[s][2]
+        size = ref.shape[1] // 2
+        return ref.at[owner, pl.ds(pl.multiple_of(core * size, 16), size)]
+
+    def quarter(s, owner, group):
+        ref = segments[s][2]
+        size = ref.shape[1] // 4
+        return ref.at[owner, pl.ds(pl.multiple_of(c * (2 * size) + group * size, 16), size)]
+
+    sent = []
+
+    def copy(ref, s, slot, peer):
+        return pltpu.make_async_remote_copy(
+            src_ref=ref,
+            dst_ref=ref,
+            send_sem=send_sem.at[s, slot],
+            recv_sem=recv_sem.at[s, slot],
+            device_id=peer,
+            device_id_type=pl.DeviceIdType.MESH,
+        )
+
+    def send(*args):
+        one = copy(*args)
+        one.start()
+        sent.append(one)
+
+    far = nz - 1
+    at_z, at_x, at_y, at_yx, at_c, at_cx = (i * far for i in range(6))
+    at_own, at_own_c = 6 * far, 6 * far + 1
+
+    def stage_own(s):
+        for d in range(far):
+            send(quarter(s, me, y), s, at_z + d, z_peer[d])
+        send(half(s, me, c), s, at_own, x_peer)
+
+    def stage_z(s):
+        for d in range(far):
+            piece = quarter(s, z_from[d] * nx + x, y)
+            copy(piece, s, at_z + d, z_peer[d]).wait_recv()
+            send(piece, s, at_x + d, x_peer)
+            send(piece, s, at_y + d, y_peer)
+
+    def stage_x(s):
+        piece = half(s, z * nx + 1 - x, c)
+        copy(piece, s, at_own, x_peer).wait_recv()
+        send(piece, s, at_own_c, c_peer)
+        for d in range(far):
+            piece = quarter(s, z_from[d] * nx + 1 - x, y)
+            copy(piece, s, at_x + d, x_peer).wait_recv()
+            send(piece, s, at_yx + d, y_peer)
+
+    def stage_y(s):
+        for d in range(far):
+            for at_from, at_to, column in ((at_y, at_c, x), (at_yx, at_cx, 1 - x)):
+                owner = z_from[d] * nx + column
+                copy(quarter(s, owner, 1 - y), s, at_from + d, y_peer).wait_recv()
+                send(half(s, owner, c), s, at_to + d, c_peer)
+
+    def stage_c(s):
+        copy(half(s, z * nx + 1 - x, 1 - c), s, at_own_c, c_peer).wait_recv()
+        for d in range(far):
+            for at, column in ((at_c, x), (at_cx, 1 - x)):
+                copy(half(s, z_from[d] * nx + column, 1 - c), s, at + d, c_peer).wait_recv()
+
+    def row_copy(b, way):
+        reach = min(2**b, nz // 2)
+        step = reach if way == 0 else -reach
+        there = z + step
+        back = z - step
+        one = pltpu.make_async_remote_copy(
+            src_ref=rows.at[b, 1],
+            dst_ref=rows.at[b, 2 * way],
+            send_sem=row_send.at[b, way],
+            recv_sem=row_recv.at[b, way],
+            device_id={"seq": lax.rem(there + nz, nz)},
+            device_id_type=pl.DeviceIdType.MESH,
+        )
+        return one, (there >= 0) & (there < nz), (back >= 0) & (back < nz)
+
+    def make_rows(b):
+        rows[b, 1] = normalize(state[...], conv_norm[b : b + 1, :]).astype(jnp.bfloat16)
+        for way in range(2):
+            _, _, receives = row_copy(b, way)
+
+            @pl.when(jnp.logical_not(receives))
+            def _():
+                rows[b, 2 * way] = jnp.zeros(rows.shape[2:], rows.dtype)
+
+    def send_rows(b):
+        for way in range(2):
+            one, sends, _ = row_copy(b, way)
+
+            @pl.when(sends)
+            def _():
+                one.start()
+
+    def wait_rows(b):
+        for way in range(2):
+            one, _, receives = row_copy(b, way)
+
+            @pl.when(receives)
+            def _():
+                one.wait_recv()
+
+    def compute(s):
+        kind, b, weights = segments[s]
+        if kind == 0:
+            wait_rows(b)
+            taps = rows.shape[1]
+            part = weights.shape[1] // taps
+            acc[...] = jnp.zeros_like(acc)
+
+            @pl.loop(0, taps)
+            def _(t):
+                piece = weights[:, pl.ds(pl.multiple_of(t * part, 16), part), :]
+                acc[...] += dot_t(rows[b, t], piece.reshape(owners * part, piece.shape[-1]))
+
+            state[...] += acc[...].astype(jnp.bfloat16).astype(jnp.float32)
+            final[...] = normalize(state[...], ff_norm[b : b + 1, :]).astype(jnp.bfloat16)
+        elif kind == 1:
+
+            @pl.loop(0, owners)
+            def _(o):
+                hidden[o] = jax.nn.gelu(matmul(final[...], weights[o])).astype(jnp.bfloat16)
+
+        else:
+
+            @pl.loop(0, owners)
+            def _(o):
+                state[...] += matmul(hidden[o], weights[o])
+
+            if b + 1 < blocks:
+                make_rows(b + 1)
+                send_rows(b + 1)
+
+    state[...] = seq_ref[...].astype(jnp.float32)
+    make_rows(0)
+    pl.semaphore_wait(barrier, len(partners))
+    send_rows(0)
+    total = len(segments)
+    for s in range(total):
+        stage_own(s)
+    for step in range(total + 3):
+        for lag, stage in enumerate((stage_z, stage_x, stage_y, stage_c)):
+            if 0 <= step - lag < total:
+                stage(step - lag)
+        if step >= 3:
+            compute(step - 3)
+
+    final[...] = normalize(state[...], head_norm[...]).astype(jnp.bfloat16)
+    swap = pltpu.make_async_remote_copy(
+        src_ref=final,
+        dst_ref=opposite,
+        send_sem=last_send,
+        recv_sem=last_recv,
+        device_id=mirror,
+        device_id_type=pl.DeviceIdType.MESH,
+    )
+    swap.start()
+    acc[...] = matmul(final[...], value_ref[...])
+    place = lax.broadcasted_iota(jnp.int32, (count, count), 0) + lax.broadcasted_iota(jnp.int32, (count, count), 1)
+    turn = jnp.where(place == count - 1, 1.0, 0.0).astype(jnp.bfloat16)
+    for one in sent:
+        one.wait_send()
+    for b in range(blocks):
+        for way in range(2):
+            one, sends, _ = row_copy(b, way)
+
+            @pl.when(sends)
+            def _():
+                one.wait_send()
+
+    swap.wait()
+    logits = matmul(opposite[...], gate_ref[...]).astype(jnp.bfloat16)
+    mirrored = matmul(turn, logits)
+    gated = (acc[...] * jax.nn.sigmoid(mirrored)).astype(jnp.bfloat16)
+    out_ref[...] = matmul(gated, out_weight[...]).astype(jnp.bfloat16)
+
+
+def fused(
+    nz,
+    nx,
+    seq_in,
+    conv_norm,
+    conv_weight,
+    ff_norm,
+    up_weight,
+    down_weight,
+    head_norm,
+    value_weight,
+    gate_weight,
+    out_weight,
+):
+    count, width = seq_in.shape[1:]
+    blocks, taps, _, part = conv_weight.shape
+    inner = up_weight.shape[2]
+    owners = nz * nx
+    conv = jnp.swapaxes(conv_weight, 2, 3).reshape(blocks, taps * part, width)
+    slots = 6 * (nz - 1) + 2
+    bf16, f32 = jnp.bfloat16, jnp.float32
+    result = pl.pallas_call(
+        functools.partial(fused_kernel, nz, nx),
+        out_shape=jax.ShapeDtypeStruct((count, width), bf16),
+        in_specs=[pl.BlockSpec(memory_space=pltpu.VMEM)] * 10,
+        out_specs=pl.BlockSpec(memory_space=pltpu.VMEM),
+        scratch_shapes=[
+            pltpu.VMEM((blocks, owners, taps * part, width), bf16),
+            pltpu.VMEM((blocks, owners, width, inner), bf16),
+            pltpu.VMEM((blocks, owners, inner, width), bf16),
+            pltpu.VMEM((count, width), f32),
+            pltpu.VMEM((count, width), f32),
+            pltpu.VMEM((owners, count, inner), bf16),
+            pltpu.VMEM((blocks, 3, count, width), bf16),
+            pltpu.VMEM((count, width), bf16),
+            pltpu.VMEM((count, width), bf16),
+            pltpu.SemaphoreType.DMA((3 * blocks, slots)),
+            pltpu.SemaphoreType.DMA((3 * blocks, slots)),
+            pltpu.SemaphoreType.DMA((blocks, 2)),
+            pltpu.SemaphoreType.DMA((blocks, 2)),
+            pltpu.SemaphoreType.DMA,
+            pltpu.SemaphoreType.DMA,
+        ],
+        compiler_params=pltpu.CompilerParams(
+            collective_id=0, has_side_effects=True, vmem_limit_bytes=40 * 2**20
+        ),
+    )(
+        seq_in[0],
+        conv_norm,
+        conv,
+        ff_norm,
+        up_weight,
+        down_weight,
+        head_norm[None],
+        value_weight,
+        gate_weight,
+        out_weight,
+    )
+    return result[None]
+
+
+def takes_kernel(mesh, conv_shape, up_shape, seq_shape):
+    sizes = dict(mesh.shape)
+    if any(sizes[a] != 2 for a in ("groups", "strand", "chan")) or not 2 <= sizes["seq"] <= 8:
+        return False
+    shards = sizes["seq"] * sizes["chan"]
+    conv_rows = conv_shape[1] * conv_shape[3] // shards
+    inner = up_shape[2] // shards
+    count = seq_shape[1] // (shards * sizes["groups"])
+    return conv_rows % 64 == 0 and conv_shape[3] // shards % 16 == 0 and inner % 128 == 0 and count % 16 == 0
+
+
 def solution(mesh):
     in_specs = (
         P("strand", ("groups", "seq", "chan"), None),
@@ -79,4 +390,11 @@
         P(),
     )
     out_specs = P("strand", ("groups", "seq", "chan"), None)
-    return jax.shard_map(local, mesh=mesh, in_specs=in_specs, out_specs=out_specs, check_vma=False)
+
+    def run(*args):
+        body = local
+        if takes_kernel(mesh, args[2].shape, args[4].shape, args[0].shape):
+            body = functools.partial(fused, mesh.shape["seq"], mesh.shape["chan"])
+        return jax.shard_map(body, mesh=mesh, in_specs=in_specs, out_specs=out_specs, check_vma=False)(*args)
+
+    return run

time: 377 us -> 109 us (0.29)
  waiting for transfers between devices: 319 us -> 0 us
  Pallas kernels: 0 us -> 98.5 us
  matrix products: 19.5 us -> 0 us
  starting transfers between devices: 17.8 us -> 0 us
  between operations: 13.7 us -> 0.02 us
  local copies, waits for them, and re-layouts: 5.8 us -> 10 us
    all_gather x6 -> x0, waiting for transfers between devices: 269 us -> none  [the longest x2 99.1 us: local(): lax.all_gather(down_weight[block], ('seq', 'chan'), axis=0, tiled=True)]
    pallas_call x0 -> x1, Pallas kernels: none -> 98.5 us  [fused(): pl.pallas_call(functools.partial(fused_kernel, nz, nx), out_shape=jax.Sha...]
    ppermute x8 -> x0, waiting for transfers between devices: 48.7 us -> none  [the longest x4 38.1 us: swapped(): lax.ppermute(x, axis, [(i, i ^ 1 << stride) for i in range(lax.axis_size(...]
    dot_general x10 -> x0, matrix products: 19.5 us -> none  [matmul(): return jnp.dot(left, right, preferred_element_type=jnp.float32)]
    ppermute x8 -> x0, starting transfers between devices: 17.6 us -> none  [the longest x4 13.7 us: passed_along(): lax.ppermute(value, axis, [(source, source + steps) for source in range(i...]
    unnamed x16 -> x21, local copies, waits for them, and re-layouts: 0.73 us -> 10 us
    slice x5 -> x0, local copies, waits for them, and re-layouts: 4.62 us -> none  [the longest x1 1.92 us: local(): conv_weight[block]]
  transfers between devices with their start and end apart: 14 -> 0, of which waited for: 11 -> 0; matrix products, arithmetic and copies ran while one was open for 4% -> 0% of each run, Pallas kernels for 0% -> 0%
where the time goes in v1:
time: 109 us; the launch traced here: 108 us
  Pallas kernels  98.5 us (90%)
  local copies, waits for them, and re-layouts  10 us (9%)
    pallas_call x1, Pallas kernels, fused(): pl.pallas_call(functools.partial(fused_kernel, nz, nx), out_shape=jax.Sha...  98.5 us
    unnamed x21, local copies, waits for them, and re-layouts  10 us

profile of v1, /device:TPU:0, one launch (start us, length us, event | category | flops | bytes accessed | tf_op | source)
XLA Modules:
  0.0 108.5 jit_solution(7506023585712889759)
XLA Ops:
  0.0 0.0 copy-start.7
  0.0 0.7 copy-done.7
  0.7 0.0 copy-start
  0.7 1.0 copy-done
  1.7 0.0 copy-start.1
  1.7 1.0 copy-done.1
  2.8 0.0 copy-start.2
  2.8 1.0 copy-done.2
  3.8 0.0 copy-start.3
  3.8 1.0 copy-done.3
  4.9 0.0 copy-start.4
  4.9 1.0 copy-done.4
  5.9 0.0 copy-start.5
  5.9 1.0 copy-done.5
  6.9 0.0 copy-start.6
  6.9 1.0 copy-done.6
  7.9 0.0 copy-start.8
  7.9 0.7 copy-done.8
  8.6 0.0 copy-start.9
  8.6 0.7 copy-done.9
  9.3 98.5 %shard_map.100 = bf16[384,512]{1,0:T(8,128)(2,1)S(1)} custom-call(bf16[384,512]{1,0:T(8,128)(2,1)S(1)} %bitcast.7, f32[2,512]{1,0:T(2,128)S(1)} %copy-done.7, bf16[2,192,512]{2,1,0:T(8,128)(2,1)S(1)} %bitcast.8, f32[2,512]{1,0:T(2,128)S(1)} %copy-done.8, bf16[2,512,256]{2,1,0:T(8,128)(2,1)S(1)} %copy-done, bf16[2,256,512]{2,1,0:T(8,128)(2,1)S(1)} %copy-done.1, ...), custom_call_target="tpu_custom_call" | custom-call | tf_op jit(solution)/shard_map/pallas_call | solution.py:328
  107.7 0.7 copy.12
Async XLA Ops:
  0.0 0.7 copy-start.7
  0.7 1.0 copy-start
  1.7 1.0 copy-start.1
  2.8 1.0 copy-start.2
  3.8 1.0 copy-start.3
  4.9 1.0 copy-start.4
  5.9 1.0 copy-start.5
  6.9 1.0 copy-start.6
  7.9 0.7 copy-start.8
  8.6 0.7 copy-start.9

commit v2 on v1

--- a/solution.py
+++ b/solution.py
@@ -76,17 +76,26 @@
 def fused_kernel(
     nz,
     nx,
+    seq_in,
+    conv_norm_in,
+    conv_ref,
+    ff_norm_in,
+    up_ref,
+    down_ref,
+    head_norm_in,
+    value_in,
+    gate_in,
+    out_in,
+    out_ref,
     seq_ref,
     conv_norm,
-    conv_ref,
     ff_norm,
-    up_ref,
-    down_ref,
     head_norm,
     value_ref,
     gate_ref,
     out_weight,
-    out_ref,
+    own_sem,
+    small_sem,
     conv_all,
     up_all,
     down_all,
@@ -109,36 +118,59 @@
     me = z * nx + x
     count = rows.shape[2]
     mirror = {"seq": nz - 1 - z, "strand": 1 - c, "chan": nx - 1 - x}
-    z_peer = [{"seq": lax.rem(z + d, nz)} for d in range(1, nz)]
+    z_from = [lax.bitwise_xor(z, d) for d in range(1, nz)]
+    z_peer = [{"seq": one} for one in z_from]
     x_peer, y_peer, c_peer = {"chan": 1 - x}, {"groups": 1 - y}, {"strand": 1 - c}
-    z_from = [lax.rem(z + nz - d, nz) for d in range(1, nz)]
 
     partners = z_peer + [x_peer, y_peer, c_peer, mirror]
     barrier = pltpu.get_barrier_semaphore()
     for peer in partners:
         pl.semaphore_signal(barrier, inc=1, device_id=peer, device_id_type=pl.DeviceIdType.MESH)
 
+    small = [
+        pltpu.make_async_copy(source, target, small_sem.at[i])
+        for i, (source, target) in enumerate(
+            (
+                (seq_in, seq_ref),
+                (conv_norm_in, conv_norm),
+                (ff_norm_in, ff_norm),
+                (head_norm_in, head_norm),
+                (value_in, value_ref),
+                (gate_in, gate_ref),
+                (out_in, out_weight),
+            )
+        )
+    ]
+    for one in small[:3]:
+        one.start()
     segments = []
+    own_copy = []
     for b in range(blocks):
         for kind, (whole, own) in enumerate(((conv_all, conv_ref), (up_all, up_ref), (down_all, down_ref))):
-            whole[b, me] = own[b]
-            segments.append((kind, b, whole.at[b]))
+            segments.append((kind, b, whole.at[b], own.at[b]))
+            own_copy.append(pltpu.make_async_copy(own.at[b], whole.at[b, me], own_sem.at[len(own_copy)]))
+    for one in own_copy + small[3:]:
+        one.start()
+
+    def half_rows(s, core):
+        size = segments[s][3].shape[0] // 2
+        return pl.ds(pl.multiple_of(core * size, 16), size)
+
+    def quarter_rows(s, group):
+        size = segments[s][3].shape[0] // 4
+        return pl.ds(pl.multiple_of(c * (2 * size) + group * size, 16), size)
 
     def half(s, owner, core):
-        ref = segments[s][2]
-        size = ref.shape[1] // 2
-        return ref.at[owner, pl.ds(pl.multiple_of(core * size, 16), size)]
+        return segments[s][2].at[owner, half_rows(s, core)]
 
     def quarter(s, owner, group):
-        ref = segments[s][2]
-        size = ref.shape[1] // 4
-        return ref.at[owner, pl.ds(pl.multiple_of(c * (2 * size) + group * size, 16), size)]
+        return segments[s][2].at[owner, quarter_rows(s, group)]
 
     sent = []
 
-    def copy(ref, s, slot, peer):
+    def copy(ref, s, slot, peer, source=None):
         return pltpu.make_async_remote_copy(
-            src_ref=ref,
+            src_ref=ref if source is None else source,
             dst_ref=ref,
             send_sem=send_sem.at[s, slot],
             recv_sem=recv_sem.at[s, slot],
@@ -157,15 +189,24 @@
 
     def stage_own(s):
         for d in range(far):
-            send(quarter(s, me, y), s, at_z + d, z_peer[d])
-        send(half(s, me, c), s, at_own, x_peer)
+            if d == 0:
+                send(half(s, me, c), s, at_z, z_peer[0], segments[s][3].at[half_rows(s, c)])
+            else:
+                send(quarter(s, me, y), s, at_z + d, z_peer[d], segments[s][3].at[quarter_rows(s, y)])
+        send(half(s, me, c), s, at_own, x_peer, segments[s][3].at[half_rows(s, c)])
 
     def stage_z(s):
         for d in range(far):
-            piece = quarter(s, z_from[d] * nx + x, y)
-            copy(piece, s, at_z + d, z_peer[d]).wait_recv()
+            owner = z_from[d] * nx + x
+            piece = quarter(s, owner, y)
+            if d == 0:
+                whole = half(s, owner, c)
+                copy(whole, s, at_z, z_peer[0]).wait_recv()
+                send(whole, s, at_c, c_peer)
+            else:
+                copy(piece, s, at_z + d, z_peer[d]).wait_recv()
+                send(piece, s, at_y + d, y_peer)
             send(piece, s, at_x + d, x_peer)
-            send(piece, s, at_y + d, y_peer)
 
     def stage_x(s):
         piece = half(s, z * nx + 1 - x, c)
@@ -179,6 +220,8 @@
     def stage_y(s):
         for d in range(far):
             for at_from, at_to, column in ((at_y, at_c, x), (at_yx, at_cx, 1 - x)):
+                if d == 0 and column is x:
+                    continue
                 owner = z_from[d] * nx + column
                 copy(quarter(s, owner, 1 - y), s, at_from + d, y_peer).wait_recv()
                 send(half(s, owner, c), s, at_to + d, c_peer)
@@ -206,10 +249,10 @@
 
     def make_rows(b):
         rows[b, 1] = normalize(state[...], conv_norm[b : b + 1, :]).astype(jnp.bfloat16)
-        for way in range(2):
-            _, _, receives = row_copy(b, way)
-
-            @pl.when(jnp.logical_not(receives))
+        reach = min(2**b, nz // 2)
+        for way, empty in ((0, z < reach), (1, z + reach >= nz)):
+
+            @pl.when(empty)
             def _():
                 rows[b, 2 * way] = jnp.zeros(rows.shape[2:], rows.dtype)
 
@@ -230,7 +273,8 @@
                 one.wait_recv()
 
     def compute(s):
-        kind, b, weights = segments[s]
+        kind, b, weights, _ = segments[s]
+        own_copy[s].wait()
         if kind == 0:
             wait_rows(b)
             taps = rows.shape[1]
@@ -260,20 +304,28 @@
                 make_rows(b + 1)
                 send_rows(b + 1)
 
+    for one in small[:3]:
+        one.wait()
     state[...] = seq_ref[...].astype(jnp.float32)
     make_rows(0)
     pl.semaphore_wait(barrier, len(partners))
     send_rows(0)
     total = len(segments)
-    for s in range(total):
+    for s in range(2):
         stage_own(s)
     for step in range(total + 3):
-        for lag, stage in enumerate((stage_z, stage_x, stage_y, stage_c)):
+        for lag, stage in ((2, stage_y), (1, stage_x), (0, stage_z), (3, stage_c)):
             if 0 <= step - lag < total:
                 stage(step - lag)
+            if lag == 0 and step + 2 < total:
+                stage_own(step + 2)
         if step >= 3:
-            compute(step - 3)
-
+            for s in range(total):
+                if s + 3 == step:
+                    compute(s)
+
+    for one in small[3:]:
+        one.wait()
     final[...] = normalize(state[...], head_norm[...]).astype(jnp.bfloat16)
     swap = pltpu.make_async_remote_copy(
         src_ref=final,
@@ -328,9 +380,18 @@
     result = pl.pallas_call(
         functools.partial(fused_kernel, nz, nx),
         out_shape=jax.ShapeDtypeStruct((count, width), bf16),
-        in_specs=[pl.BlockSpec(memory_space=pltpu.VMEM)] * 10,
+        in_specs=[pl.BlockSpec(memory_space=pltpu.HBM)] * 10,
         out_specs=pl.BlockSpec(memory_space=pltpu.VMEM),
         scratch_shapes=[
+            pltpu.VMEM((count, width), bf16),
+            pltpu.VMEM(conv_norm.shape, f32),
+            pltpu.VMEM(ff_norm.shape, f32),
+            pltpu.VMEM((1, width), f32),
+            pltpu.VMEM(value_weight.shape, bf16),
+            pltpu.VMEM(gate_weight.shape, bf16),
+            pltpu.VMEM(out_weight.shape, bf16),
+            pltpu.SemaphoreType.DMA((3 * blocks,)),
+            pltpu.SemaphoreType.DMA((7,)),
             pltpu.VMEM((blocks, owners, taps * part, width), bf16),
             pltpu.VMEM((blocks, owners, width, inner), bf16),
             pltpu.VMEM((blocks, owners, inner, width), bf16),
@@ -348,7 +409,7 @@
             pltpu.SemaphoreType.DMA,
         ],
         compiler_params=pltpu.CompilerParams(
-            collective_id=0, has_side_effects=True, vmem_limit_bytes=40 * 2**20
+            collective_id=0, has_side_effects=True, vmem_limit_bytes=60 * 2**20
         ),
     )(
         seq_in[0],

time: 109 us -> 92.7 us (0.85)
  local copies, waits for them, and re-layouts: 10 us -> 1.77 us
  Pallas kernels: 98.5 us -> 90.8 us
    unnamed x21 -> x1, local copies, waits for them, and re-layouts: 10 us -> 1.77 us
    pallas_call x1, Pallas kernels: 98.5 us -> 90.8 us  [fused(): pl.pallas_call(functools.partial(fused_kernel, nz, nx), out_shape=jax.Sha...]
where the time goes in v2:
time: 92.7 us; the launch traced here: 92.5 us
  Pallas kernels  90.8 us (98%)
  local copies, waits for them, and re-layouts  1.77 us (2%)
    pallas_call x1, Pallas kernels, fused(): pl.pallas_call(functools.partial(fused_kernel, nz, nx), out_shape=jax.Sha...  90.8 us

profile of v2, /device:TPU:0, one launch (start us, length us, event | category | flops | bytes accessed | tf_op | source)
XLA Modules:
  0.0 92.5 jit_solution(12970411580132782052)
XLA Ops:
  0.0 90.8 %shard_map.100 = bf16[384,512]{1,0:T(8,128)(2,1)} custom-call(bf16[384,512]{1,0:T(8,128)(2,1)} %bitcast.7, f32[2,512]{1,0:T(2,128)} %conv_norm_in.1, bf16[2,192,512]{2,1,0:T(8,128)(2,1)} %bitcast.8, f32[2,512]{1,0:T(2,128)} %ff_norm_in.1, bf16[2,512,256]{2,1,0:T(8,128)(2,1)} %up_ref.1, bf16[2,256,512]{2,1,0:T(8,128)(2,1)} %down_ref.1, f32[1,512]{1,0:T(1,128)} %bitcast.9, ...), custom_call_target="tpu_custom_call" | custom-call | tf_op jit(solution)/shard_map/pallas_call | solution.py:380
  90.8 1.8 %copy.12 = bf16[1,384,512]{2,1,0:T(8,128)(2,1)} copy(bf16[1,384,512]{2,1,0:T(8,128)(2,1)} %bitcast.6) | data formatting | bytes 786432

commit v3 on v2

--- a/solution.py
+++ b/solution.py
@@ -272,19 +272,34 @@
             def _():
                 one.wait_recv()
 
+    cuts = last_send.shape[0]
+    cut = count // cuts
+    spans = [pl.ds(i * cut, cut) for i in range(cuts)]
+    swaps = [
+        pltpu.make_async_remote_copy(
+            src_ref=final.at[span],
+            dst_ref=opposite.at[span],
+            send_sem=last_send.at[i],
+            recv_sem=last_recv.at[i],
+            device_id=mirror,
+            device_id_type=pl.DeviceIdType.MESH,
+        )
+        for i, span in enumerate(spans)
+    ]
+
     def compute(s):
         kind, b, weights, _ = segments[s]
         own_copy[s].wait()
         if kind == 0:
+            part = weights.shape[1] // rows.shape[1]
+            piece = weights[:, part : 2 * part, :]
+            acc[...] = dot_t(rows[b, 1], piece.reshape(owners * part, piece.shape[-1]))
             wait_rows(b)
-            taps = rows.shape[1]
-            part = weights.shape[1] // taps
-            acc[...] = jnp.zeros_like(acc)
-
-            @pl.loop(0, taps)
-            def _(t):
-                piece = weights[:, pl.ds(pl.multiple_of(t * part, 16), part), :]
-                acc[...] += dot_t(rows[b, t], piece.reshape(owners * part, piece.shape[-1]))
+
+            @pl.loop(0, 2)
+            def _(side):
+                piece = weights[:, pl.ds(pl.multiple_of(side * (2 * part), 16), part), :]
+                acc[...] += dot_t(rows[b, 2 * side], piece.reshape(owners * part, piece.shape[-1]))
 
             state[...] += acc[...].astype(jnp.bfloat16).astype(jnp.float32)
             final[...] = normalize(state[...], ff_norm[b : b + 1, :]).astype(jnp.bfloat16)
@@ -294,15 +309,26 @@
             def _(o):
                 hidden[o] = jax.nn.gelu(matmul(final[...], weights[o])).astype(jnp.bfloat16)
 
-        else:
+        elif b + 1 < blocks:
 
             @pl.loop(0, owners)
             def _(o):
                 state[...] += matmul(hidden[o], weights[o])
 
-            if b + 1 < blocks:
-                make_rows(b + 1)
-                send_rows(b + 1)
+            make_rows(b + 1)
+            send_rows(b + 1)
+        else:
+            for one in small[3:]:
+                one.wait()
+            for i, swap in enumerate(swaps):
+                span = spans[i]
+
+                @pl.loop(0, owners)
+                def _(o):
+                    state[span, :] += matmul(hidden[o, span, :], weights[o])
+
+                final[span, :] = normalize(state[span, :], head_norm[...]).astype(jnp.bfloat16)
+                swap.start()
 
     for one in small[:3]:
         one.wait()
@@ -311,34 +337,22 @@
     pl.semaphore_wait(barrier, len(partners))
     send_rows(0)
     total = len(segments)
-    for s in range(2):
+    for s in range(3):
         stage_own(s)
     for step in range(total + 3):
         for lag, stage in ((2, stage_y), (1, stage_x), (0, stage_z), (3, stage_c)):
             if 0 <= step - lag < total:
                 stage(step - lag)
-            if lag == 0 and step + 2 < total:
-                stage_own(step + 2)
+            if lag == 0 and step + 3 < total:
+                stage_own(step + 3)
         if step >= 3:
             for s in range(total):
                 if s + 3 == step:
                     compute(s)
 
-    for one in small[3:]:
-        one.wait()
-    final[...] = normalize(state[...], head_norm[...]).astype(jnp.bfloat16)
-    swap = pltpu.make_async_remote_copy(
-        src_ref=final,
-        dst_ref=opposite,
-        send_sem=last_send,
-        recv_sem=last_recv,
-        device_id=mirror,
-        device_id_type=pl.DeviceIdType.MESH,
-    )
-    swap.start()
     acc[...] = matmul(final[...], value_ref[...])
-    place = lax.broadcasted_iota(jnp.int32, (count, count), 0) + lax.broadcasted_iota(jnp.int32, (count, count), 1)
-    turn = jnp.where(place == count - 1, 1.0, 0.0).astype(jnp.bfloat16)
+    place = lax.broadcasted_iota(jnp.int32, (cut, cut), 0) + lax.broadcasted_iota(jnp.int32, (cut, cut), 1)
+    turn = jnp.where(place == cut - 1, 1.0, 0.0).astype(jnp.bfloat16)
     for one in sent:
         one.wait_send()
     for b in range(blocks):
@@ -349,11 +363,13 @@
             def _():
                 one.wait_send()
 
-    swap.wait()
-    logits = matmul(opposite[...], gate_ref[...]).astype(jnp.bfloat16)
-    mirrored = matmul(turn, logits)
-    gated = (acc[...] * jax.nn.sigmoid(mirrored)).astype(jnp.bfloat16)
-    out_ref[...] = matmul(gated, out_weight[...]).astype(jnp.bfloat16)
+    for i, swap in enumerate(swaps):
+        swap.wait()
+        logits = matmul(opposite[spans[i], :], gate_ref[...]).astype(jnp.bfloat16)
+        mirrored = matmul(turn, logits)
+        span = spans[cuts - 1 - i]
+        gated = (acc[span, :] * jax.nn.sigmoid(mirrored)).astype(jnp.bfloat16)
+        out_ref[span, :] = matmul(gated, out_weight[...]).astype(jnp.bfloat16)
 
 
 def fused(
@@ -405,8 +421,8 @@
             pltpu.SemaphoreType.DMA((3 * blocks, slots)),
             pltpu.SemaphoreType.DMA((blocks, 2)),
             pltpu.SemaphoreType.DMA((blocks, 2)),
-            pltpu.SemaphoreType.DMA,
-            pltpu.SemaphoreType.DMA,
+            pltpu.SemaphoreType.DMA((3,)),
+            pltpu.SemaphoreType.DMA((3,)),
         ],
         compiler_params=pltpu.CompilerParams(
             collective_id=0, has_side_effects=True, vmem_limit_bytes=60 * 2**20
@@ -434,7 +450,7 @@
     conv_rows = conv_shape[1] * conv_shape[3] // shards
     inner = up_shape[2] // shards
     count = seq_shape[1] // (shards * sizes["groups"])
-    return conv_rows % 64 == 0 and conv_shape[3] // shards % 16 == 0 and inner % 128 == 0 and count % 16 == 0
+    return conv_rows % 64 == 0 and conv_shape[3] // shards % 16 == 0 and inner % 128 == 0 and count % 48 == 0
 
 
 def solution(mesh):

time: 92.7 us -> 90.3 us (0.974); the launches traced: 92.5 us -> 88.6 us
  Pallas kernels: 90.8 us -> 86.8 us
    pallas_call x1, Pallas kernels: 90.8 us -> 86.8 us  [fused(): pl.pallas_call(functools.partial(fused_kernel, nz, nx), out_shape=jax.Sha...]
where the time goes in v3:
time: 90.3 us; the launch traced here: 88.6 us
  Pallas kernels  86.8 us (96%)
  local copies, waits for them, and re-layouts  1.77 us (2%)
    pallas_call x1, Pallas kernels, fused(): pl.pallas_call(functools.partial(fused_kernel, nz, nx), out_shape=jax.Sha...  86.8 us

profile of v3, /device:TPU:0, one launch (start us, length us, event | category | flops | bytes accessed | tf_op | source)
XLA Modules:
  0.0 88.6 jit_solution(5082829070750569461)
XLA Ops:
  0.0 86.8 %shard_map.100 = bf16[384,512]{1,0:T(8,128)(2,1)} custom-call(bf16[384,512]{1,0:T(8,128)(2,1)} %bitcast.7, f32[2,512]{1,0:T(2,128)} %conv_norm_in.1, bf16[2,192,512]{2,1,0:T(8,128)(2,1)} %bitcast.8, f32[2,512]{1,0:T(2,128)} %ff_norm_in.1, bf16[2,512,256]{2,1,0:T(8,128)(2,1)} %up_ref.1, bf16[2,256,512]{2,1,0:T(8,128)(2,1)} %down_ref.1, f32[1,512]{1,0:T(1,128)} %bitcast.9, ...), custom_call_target="tpu_custom_call" | custom-call | tf_op jit(solution)/shard_map/pallas_call | solution.py:396
  86.8 1.8 %copy.12 = bf16[1,384,512]{2,1,0:T(8,128)(2,1)} copy(bf16[1,384,512]{2,1,0:T(8,128)(2,1)} %bitcast.6) | data formatting | bytes 786432
